TPU v7x, 128 devices: a whole 4x4x4 slice. The times are simulated.
128 devices in a mesh: outer: 8 (over y, core), inner: 16 (over z, x).
Axes of the slice: x: 4, y: 4, z: 4, core: 2. Of those that a mesh axis runs over, the one named last changes fastest.
Arguments:
- byte_states: bfloat16 [65536, 1024], P(('outer', 'inner')), may hold values from -6 to 6
- patch_vectors: bfloat16 [16384, 1024], P(('outer', 'inner')), may hold values from -6 to 6
- patch_starts: int32 [16384], P(('outer', 'inner')), may hold values from 0 to 65535, as said below
- beta_codes: int32 [65536, 8], P(('outer', 'inner')), may hold values from 0 to 8, as said below
- w_qkv: bfloat16 [1024, 3072], replicated, may hold values from -0.1875 to 0.1875
- conv_taps: float32 [4, 3072], replicated, may hold values from -3 to 3
- norm_gain: float32 [1024], replicated, may hold values from 0.5 to 1.5
- w_out: bfloat16 [1024, 1024], replicated, may hold values from -0.1875 to 0.1875
Outputs:
- mixed_bytes: bfloat16 [65536, 1024], P(('outer', 'inner'))
Inputs may be any that keep to these rules, and one draw needn't show every extreme that they name: `patch_starts`: strictly increasing; entries j * 128 to (j + 1) * 128 - 1 lie in [j * 512, (j + 1) * 512); the first entry is 0. `beta_codes`: code c stands for beta = c / 4.
All inputs are finite; a program needn't handle non-finite values.
Results may differ from a plain program's by a relative error of at most 0.012.
The roundings to bfloat16 on the way count: a program that leaves them out, or rounds other values in their place, can miss the bound.
Values may be sent and summed in bfloat16 or wider, within the bound.
A program may use at most 320 MiB of HBM per device.

v0:
```python
import jax
import jax.numpy as jnp
from jax import lax
from jax.sharding import PartitionSpec as P

SPAN = 128


exact_arithmetic_mode = lax.Precision.HIGHEST
norm_eps = 1e-06


def shifted(value, axis, steps):
    count = lax.axis_size(axis)
    leading, last = (max(0, -steps), min(count, count - steps))
    return lax.ppermute(value, axis, [(source, source + steps) for source in range(leading, last)])


def carried_in(x, axis, combine, identity):
    length, place = (lax.axis_size(axis), lax.axis_index(axis))
    everything = jax.tree.map(lambda part: lax.all_gather(part, axis), x)
    start = jax.tree.map(
        lambda part, zero: jnp.broadcast_to(jnp.asarray(zero, part.dtype), part.shape), x, identity
    )

    def lap(k, before):
        reached = k < place
        new = combine(before, jax.tree.map(lambda part: part[k], everything))
        return jax.tree.map(lambda a, b: jnp.where(reached, a, b), new, before)

    return lax.fori_loop(0, length, lap, start)


def broadcast(x, axis, root):
    mine = lax.axis_index(axis) == root
    return lax.psum(jnp.where(mine, x, jnp.zeros_like(x)), axis)


def pair_combine(earlier, later):
    early_move, early_rest = earlier
    late_move, late_rest = later
    moved = jnp.einsum("...ij,...jk->...ik", late_move, early_move, precision=exact_arithmetic_mode)
    rested = (
        jnp.einsum("...ij,...jk->...ik", late_move, early_rest, precision=exact_arithmetic_mode)
        + late_rest
    )
    return (moved, rested)


def unit_lower_solve(lower_part, right_side):
    span_len = lower_part.shape[-1]
    block_len = 16
    block_total = span_len // block_len
    identity_block = jnp.eye(block_len, dtype=jnp.float32)
    solved_parts = []
    for block_number in range(block_total):
        low = block_number * block_len
        high = low + block_len
        diagonal_part = lower_part[..., low:high, low:high]
        inverse_part = identity_block - diagonal_part
        power_part = diagonal_part
        reach = 1
        while reach * 2 < block_len:
            power_part = jnp.einsum(
                "...ij,...jk->...ik", power_part, power_part, precision=exact_arithmetic_mode
            )
            inverse_part = jnp.einsum(
                "...ij,...jk->...ik",
                inverse_part,
                identity_block + power_part,
                precision=exact_arithmetic_mode,
            )
            reach = reach * 2
        pending = right_side[..., low:high, :]
        if block_number > 0:
            earlier_rows = jnp.concatenate(solved_parts, axis=-2)
            pending = pending - jnp.einsum(
                "...ij,...jk->...ik",
                lower_part[..., low:high, :low],
                earlier_rows,
                precision=exact_arithmetic_mode,
            )
        solved_parts.append(
            jnp.einsum("...ij,...jk->...ik", inverse_part, pending, precision=exact_arithmetic_mode)
        )
    return jnp.concatenate(solved_parts, axis=-2)


def local(byte_states, patch_vectors, patch_starts, beta_codes, w_qkv, conv_taps, norm_gain, w_out):
    tok_rows = byte_states.shape[0]
    width = byte_states.shape[1]
    head_count = beta_codes.shape[1]
    head_size = width // head_count
    span_len = SPAN
    span_count = tok_rows // span_len
    open_row = shifted(patch_vectors[patch_vectors.shape[0] - 1 :], ("outer", "inner"), 1)
    patch_table = jnp.concatenate([open_row, patch_vectors], axis=0)
    first_position = lax.axis_index(("outer", "inner")) * tok_rows
    token_positions = first_position + jnp.arange(tok_rows, dtype=jnp.int32)
    patch_index = jnp.sum(
        (patch_starts[None, :] <= token_positions[:, None]).astype(jnp.int32), axis=1
    )
    fetched = jnp.take(patch_table, patch_index, axis=0)
    hidden = (byte_states.astype(jnp.float32) + fetched.astype(jnp.float32)).astype(jnp.bfloat16)
    projected = jnp.dot(hidden, w_qkv, preferred_element_type=jnp.float32).astype(jnp.bfloat16)
    rim_rows = shifted(projected[tok_rows - 3 :], ("outer", "inner"), 1)
    extended = jnp.concatenate([rim_rows, projected], axis=0).astype(jnp.float32)
    running = jnp.zeros((tok_rows, extended.shape[1]), jnp.float32)
    for offset in range(4):
        running = running + conv_taps[offset][None, :] * extended[offset : offset + tok_rows]
    activated = jax.nn.silu(running)

    def to_spans(flat_heads):
        return flat_heads.reshape(span_count, span_len, head_count, head_size).transpose(0, 2, 1, 3)

    raw_keys = activated[:, width : 2 * width].reshape(tok_rows, head_count, head_size)
    unit_keys = raw_keys / jnp.sqrt(jnp.sum(raw_keys * raw_keys, axis=-1, keepdims=True) + norm_eps)
    query_blocks = to_spans(activated[:, :width].reshape(tok_rows, head_count, head_size))
    key_blocks = to_spans(unit_keys)
    value_blocks = to_spans(activated[:, 2 * width :].reshape(tok_rows, head_count, head_size))
    beta_blocks = (
        (beta_codes.astype(jnp.float32) * 0.25)
        .reshape(span_count, span_len, head_count)
        .transpose(0, 2, 1)
    )
    gram = jnp.einsum("nhik,nhjk->nhij", key_blocks, key_blocks, precision=exact_arithmetic_mode)
    strict_lower = jnp.tril(jnp.ones((span_len, span_len), jnp.bool_), -1)
    lower_part = jnp.where(strict_lower, beta_blocks[..., :, None] * gram, 0.0)
    right_side = beta_blocks[..., None] * jnp.concatenate([key_blocks, value_blocks], axis=-1)
    solved = unit_lower_solve(lower_part, right_side)
    w_rows = solved[..., :head_size]
    u_rows = solved[..., head_size:]
    identity_head = jnp.eye(head_size, dtype=jnp.float32)
    transitions = identity_head - jnp.einsum(
        "nhck,nhcl->nhkl", key_blocks, w_rows, precision=exact_arithmetic_mode
    )
    residues = jnp.einsum("nhck,nhcv->nhkv", key_blocks, u_rows, precision=exact_arithmetic_mode)
    level_move, level_rest = (transitions, residues)
    while level_move.shape[0] > 1:
        count_now = level_move.shape[0]
        half_count = count_now // 2
        merged_move, merged_rest = pair_combine(
            (level_move[0 : 2 * half_count : 2], level_rest[0 : 2 * half_count : 2]),
            (level_move[1 : 2 * half_count : 2], level_rest[1 : 2 * half_count : 2]),
        )
        level_move, level_rest = (merged_move, merged_rest)
    local_move = level_move[0]
    local_rest = level_rest[0]
    identity_pair = (
        jnp.broadcast_to(identity_head, (head_count, head_size, head_size)),
        jnp.zeros((head_count, head_size, head_size), jnp.float32),
    )
    inner_move, inner_rest = carried_in(
        (local_move, local_rest), "inner", pair_combine, identity_pair
    )
    upto_move, upto_rest = pair_combine((inner_move, inner_rest), (local_move, local_rest))
    stacked = jnp.concatenate([upto_move, upto_rest], axis=-1)
    group_stack = broadcast(stacked, "inner", lax.axis_size("inner") - 1)
    group_move = group_stack[..., :head_size]
    group_rest = group_stack[..., head_size:]
    outer_move, outer_rest = carried_in(
        (group_move, group_rest), "outer", pair_combine, identity_pair
    )
    start_state = (
        jnp.einsum("hij,hjk->hik", inner_move, outer_rest, precision=exact_arithmetic_mode)
        + inner_rest
    )
    causal_mask = jnp.tril(jnp.ones((span_len, span_len), jnp.bool_), 0)
    query_key = jnp.where(
        causal_mask,
        jnp.einsum("nhik,nhjk->nhij", query_blocks, key_blocks, precision=exact_arithmetic_mode),
        0.0,
    )

    def span_step(current_state, inputs):
        block_of_queries, block_of_keys, weight_block_rows, u_block, score_block = inputs
        incoming_values = u_block - jnp.einsum(
            "nty,nyg->ntg", weight_block_rows, current_state, precision=exact_arithmetic_mode
        )
        block_of_outputs = jnp.einsum(
            "nty,nyg->ntg", block_of_queries, current_state, precision=exact_arithmetic_mode
        )
        block_of_outputs = block_of_outputs + jnp.einsum(
            "hcj,hjv->hcv", score_block, incoming_values, precision=exact_arithmetic_mode
        )
        current_state = current_state + jnp.einsum(
            "isf,ist->ift", block_of_keys, incoming_values, precision=exact_arithmetic_mode
        )
        return (current_state, block_of_outputs)

    final_state, outputs = lax.scan(
        span_step, start_state, (query_blocks, key_blocks, w_rows, u_rows, query_key)
    )
    mean_square = jnp.mean(outputs * outputs, axis=-1, keepdims=True)
    gain_heads = norm_gain.reshape(head_count, head_size)
    normed = outputs / jnp.sqrt(mean_square + norm_eps) * gain_heads[None, :, None, :]
    normed = normed.transpose(0, 2, 1, 3).reshape(tok_rows, width).astype(jnp.bfloat16)
    return jnp.dot(normed, w_out, preferred_element_type=jnp.float32).astype(jnp.bfloat16)


def solution(mesh):
    in_specs = (
        P(("outer", "inner"), None),
        P(("outer", "inner"), None),
        P(("outer", "inner")),
        P(("outer", "inner"), None),
        P(),
        P(),
        P(),
        P(),
    )
    out_specs = P(("outer", "inner"), None)
    return jax.shard_map(local, mesh=mesh, in_specs=in_specs, out_specs=out_specs, check_vma=False)
```

profile of v0, /device:TPU:17, one launch (start us, length us, event | category | flops | bytes accessed | tf_op | source)
XLA Modules:
  0.0 529.6 jit_solution(10209254599223954571)
XLA Ops:
  7.4 3.1 collective-permute-start
  13.9 3.2 collective-permute-done
  18.1 2.1 gather_fusion
  20.2 6.8 %convolution_convert_fusion = bf16[512,3072]{1,0:T(8,128)(2,1)S(1)} fusion(bf16[1024,3072]{1,0:T(8,128)(2,1)} %param.18, bf16[512,1024]{1,0:T(8,128)(2,1)} %param.14, bf16[512,1024]{1,0:T(8,128)(2,1)S(1)} %gather_fusion, pred[512]{0:T(512)(128)(4,1)S(1)} %compare_and_fusion), kind=kOutput, calls=%fused_computation.49 | convolution fusion | flops 3225419776 | bytes 11534848 | tf_op jit(solution)/shard_map/dot_general | solution.py:105
  27.0 1.9 collective-permute-start.1
  29.0 6.9 %collective-permute-done.1 = bf16[3,3072]{1,0:T(4,128)(2,1)S(1)} collective-permute-done((bf16[3,3072]{1,0:T(4,128)(2,1)S(1)}, bf16[3,3072]{1,0:T(4,128)(2,1)S(1)}, u32[]{:S(2)}, u32[]{:S(2)}) %collective-permute-start.1) | collective-permute-done | bytes 18464 | tf_op jit(solution)/shard_map/ppermute | solution.py:16
  36.8 4.2 divide_multiply_fusion
  41.1 3.0 slice_bitcast_fusion
  45.8 2.2 reduce_sum.31
  48.2 2.1 copy.76
  50.9 4.5 multiply_select_fusion
  87.3 1.9 convolution_subtract_fusion.4
  91.0 3.7 fusion.169
  94.7 3.7 convolution_subtract_fusion.1
  99.6 2.3 convolution_add_fusion.4
  101.9 2.0 fusion.58
  104.0 2.0 copy.63
  107.6 66.0 %all-gather.8.cloned.1.call-done = f32[16,8,128,128]{3,2,1,0:T(8,128)} async-done(((f32[1,8,128,128]{3,2,1,0:T(8,128)}), f32[16,8,128,128]{3,2,1,0:T(8,128)}) %all-gather.8.cloned.1.call-update) | async-done | bytes 8388624 | tf_op jit(solution)/shard_map/all_gather | solution.py:21
  173.6 72.6 %all-gather.10.cloned.1.call-done = f32[128,128,128]{2,1,0:T(8,128)} async-done(((f32[8,128,128]{2,1,0:T(8,128)}), f32[128,128,128]{2,1,0:T(8,128)}) %all-gather.10.cloned.1.call-update) | async-done | bytes 8388624 | tf_op jit(solution)/shard_map/all_gather | solution.py:21
  246.3 59.0 %while.46 = (s32[]{:T(128)}, f32[8,128,128]{2,1,0:T(8,128)S(1)}, f32[8,128,128]{2,1,0:T(8,128)S(1)}, s32[]{:T(128)}, f32[16,8,128,128]{3,2,1,0:T(8,128)}, /*index=5*/f32[16,8,128,128]{3,2,1,0:T(8,128)}) while((s32[]{:T(128)}, f32[8,128,128]{2,1,0:T(8,128)S(1)}, f32[8,128,128]{2,1,0:T(8,128)S(1)}, s32[]{:T(128)}, ...), condition=%wide.region_3.4_spmd.clone.clone, body=%wide.region_2.3_spmd.clone.sunk.clone | while | flops 403308544 | bytes 6818904 | solution.py:31
  246.3 1.9 fusion.335
  250.0 1.9 fusion.335
  253.7 1.9 fusion.335
  257.4 1.9 fusion.335
  261.1 1.9 fusion.335
  264.8 1.9 fusion.335
  268.5 1.9 fusion.335
  272.2 1.9 fusion.335
  275.8 1.9 fusion.335
  279.5 1.9 fusion.335
  283.2 1.9 fusion.335
  286.9 1.9 fusion.335
  290.6 1.9 fusion.335
  294.3 1.9 fusion.335
  298.0 1.9 fusion.335
  301.7 1.9 fusion.335
  305.3 2.2 fusion.191
  307.5 2.2 convolution_add_fusion.6
  311.1 85.2 %all-reduce.2.cloned.1.call-done = f32[8,128,256]{1,2,0:T(8,128)} async-done(((f32[8,128,256]{1,2,0:T(8,128)}), f32[8,128,256]{1,2,0:T(8,128)}) %all-reduce.2.cloned.1.call-update) | async-done | bytes 1048592 | tf_op jit(solution)/shard_map/psum | solution.py:36
  396.3 2.1 fusion.173
  398.3 2.1 copy.66
  401.5 2.1 copy.79
  406.6 2.6 fusion.172
  409.2 6.0 %convolution_select_fusion.1 = f32[4,8,128,128]{3,2,1,0:T(8,128)} fusion(f32[4,8,128,128]{3,2,1,0:T(8,128)S(1)} %copy-done.2, pred[128,128]{1,0:T(8,128)(4,1)S(1)} %iota_compare_fusion, f32[4,128,8,128]{3,2,1,0:T(8,128)S(1)} %bitcast.236), kind=kOutput, calls=%fused_computation.72 | convolution fusion | flops 805830656 | bytes 6307840 | tf_op jit(solution)/shard_map/nhik,nhjk->nhij/dot_general | solution.py:171
  415.2 17.2 %all-gather.12.cloned.1.call-done = f32[64,128,128]{2,1,0:T(8,128)} async-done(((f32[8,128,128]{2,1,0:T(8,128)}), f32[64,128,128]{2,1,0:T(8,128)}) %all-gather.12.cloned.1.call-update) | async-done | bytes 4194320 | tf_op jit(solution)/shard_map/all_gather | solution.py:21
  432.4 33.7 %all-gather.14.cloned.1.call-done = f32[64,128,128]{2,1,0:T(8,128)} async-done(((f32[8,128,128]{2,1,0:T(8,128)}), f32[64,128,128]{2,1,0:T(8,128)}) %all-gather.14.cloned.1.call-update) | async-done | bytes 4194320 | tf_op jit(solution)/shard_map/all_gather | solution.py:21
  466.0 15.6 %while.47 = (s32[]{:T(128)}, f32[8,128,128]{2,1,0:T(8,128)S(1)}, s32[]{:T(128)}, f32[8,8,128,128]{3,2,1,0:T(8,128)}, f32[8,8,128,128]{3,2,1,0:T(8,128)}) while((s32[]{:T(128)}, f32[8,128,128]{2,1,0:T(8,128)S(1)}, s32[]{:T(128)}, f32[8,8,128,128]{3,2,1,0:T(8,128)}, f32[8,8,128,128]{3,2,1,0:T(8,128)}) %tuple.143), condition=%wide.region_6.7_spmd.clone.clone, body=%wide.region_5.6_spmd.clone.sunk.clone | while | flops 201850880 | bytes 3672655 | solution.py:31
  466.1 1.9 fusion.338
  468.0 1.9 fusion.338
  470.0 1.9 fusion.338
  471.9 1.9 fusion.338
  473.9 1.9 fusion.338
  479.7 1.9 fusion.338
  484.2 32.5 %while.45 = (s32[]{:T(128)}, f32[8,128,128]{2,1,0:T(8,128)S(1)}, f32[4,8,128,128]{3,2,1,0:T(8,128)}, f32[4,8,128,128]{3,2,1,0:T(8,128)}, f32[4,8,128,128]{3,2,1,...) while((s32[]{:T(128)}, f32[8,128,128]{2,1,0:T(8,128)S(1)}, ...), condition=%wide.region_8.9_spmd.clone, body=%wide.region_7.8_spmd.sunk.clone | while | flops 805699584 | bytes 7867477 | solution.py:191
  487.8 2.5 fusion.330
  490.3 2.1 convolution_add_fusion.17
  495.9 2.5 fusion.330
  498.4 2.1 convolution_add_fusion.17
  504.1 2.5 fusion.330
  506.6 2.1 convolution_add_fusion.17
  512.2 2.5 fusion.330
  514.7 2.1 convolution_add_fusion.17
  516.8 2.3 multiply_reduce_fusion
  520.6 2.2 convolution_convert_fusion.1
  (198 shorter events, 100.5 us)
Async XLA Ops:
  6.5 514.1 %copy-start = (bf16[1024,1024]{1,0:T(8,128)(2,1)S(1)}, bf16[1024,1024]{1,0:T(8,128)(2,1)}, u32[]{:S(2)}) copy-start(bf16[1024,1024]{1,0:T(8,128)(2,1)} %param.21) | copy-start | bytes 6291460
  6.5 167.1 %all-gather.8.cloned.1.call-start = ((), (), s32[]{:S(2)}) async-start(), calls=%async_computation | async-start | bytes 8912896 | tf_op jit(solution)/shard_map/all_gather | solution.py:21
  7.4 9.7 %collective-permute-start = (bf16[1,1024]{1,0:T(2,128)(2,1)S(1)}, bf16[1,1024]{1,0:T(2,128)(2,1)S(1)}, u32[]{:S(2)}, u32[]{:S(2)}) collective-permute-start(bf16[1,1024]{1,0:T(2,128)(2,1)S(1)} %slice.149), channel_id=1, source_target_pairs={{0,1},{1,2},{2,3},{3,4},{4,5},{5,6},{6,7},{7,8},{8,9},{9,10},{10,1... | collective-permute-start | bytes 6152 | tf_op jit(solution)/shard_map/ppermute | solution.py:16
  27.0 8.9 %collective-permute-start.1 = (bf16[3,3072]{1,0:T(4,128)(2,1)S(1)}, bf16[3,3072]{1,0:T(4,128)(2,1)S(1)}, u32[]{:S(2)}, u32[]{:S(2)}) collective-permute-start(bf16[3,3072]{1,0:T(4,128)(2,1)S(1)} %slice.198), channel_id=1, source_target_pairs={{0,1},{1,2},{2,3},{3,4},{4,5},{5,6},{6,7},{7,8},{8,9},{9,10},{10,1... | collective-permute-start | bytes 55304 | tf_op jit(solution)/shard_map/ppermute | solution.py:16
  28.9 7.9 %copy-start.9 = (f32[1,3072]{1,0:T(1,128)S(1)}, f32[1,3072]{1,0:T(1,128)}, u32[]{:S(2)}) copy-start(f32[1,3072]{1,0:T(1,128)} %get-tuple-element.429) | copy-start | bytes 36868
  29.0 7.9 %copy-start.10 = (f32[1,3072]{1,0:T(1,128)S(1)}, f32[1,3072]{1,0:T(1,128)}, u32[]{:S(2)}) copy-start(f32[1,3072]{1,0:T(1,128)} %get-tuple-element.430) | copy-start | bytes 36868
  50.9 43.8 %copy-start.1 = (f32[4,8,128,128]{3,2,1,0:T(8,128)}, f32[4,8,128,128]{3,2,1,0:T(8,128)S(1)}, u32[]{:S(2)}) copy-start(f32[4,8,128,128]{3,2,1,0:T(8,128)S(1)} %fusion.45) | copy-start | bytes 6291460
  64.5 2.5 copy-start.7
  91.0 3.7 copy-start.4
  106.0 140.2 %all-gather.10.cloned.1.call-start = ((), (), s32[]{:S(2)}) async-start(), calls=%async_computation.2 | async-start | bytes 8912896 | tf_op jit(solution)/shard_map/all_gather | solution.py:21
  107.5 288.7 %all-reduce.2.cloned.1.call-start = ((), (), s32[]{:S(2)}) async-start(), calls=%async_computation.1 | async-start | bytes 2097152 | tf_op jit(solution)/shard_map/psum | solution.py:36
  305.3 5.5 %copy-start.3 = (f32[8,128,128]{2,1,0:T(8,128)}, f32[8,128,128]{2,1,0:T(8,128)S(1)}, u32[]{:S(2)}) copy-start(f32[8,128,128]{2,1,0:T(8,128)S(1)} %get-tuple-element.252) | copy-start | bytes 1572868
  310.8 121.6 %all-gather.12.cloned.1.call-start = ((), (), s32[]{:S(2)}) async-start(), calls=%async_computation.3 | async-start | bytes 4718592 | tf_op jit(solution)/shard_map/all_gather | solution.py:21
  400.4 65.6 %all-gather.14.cloned.1.call-start = ((), (), s32[]{:S(2)}) async-start(), calls=%async_computation.4 | async-start | bytes 4718592 | tf_op jit(solution)/shard_map/all_gather | solution.py:21
  403.6 2.9 copy-start.5
  406.6 2.6 copy-start.2
  481.6 0.8 copy-start.6
  516.8 2.4 copy-start.8
  516.8 2.4 copy-start.11
Sparse Core Ops, SparseCore 0:
  106.1 67.4 all-gather.7
  175.8 70.4 all-gather.9
  310.9 85.2 all-reduce.1
  400.6 31.7 all-gather.11
  433.9 32.0 all-gather.13
where the time goes:
time: 539 us; the launch traced here: 530 us
  waiting for transfers between devices  285 us (53%)
  matrix products  178 us (33%)
  local copies, waits for them, and re-layouts  27.1 us (5%)
  other arithmetic  18.6 us (3%)
  between operations  14.3 us (3%)
  starting transfers between devices  5.41 us (1%)
    all_gather x4, waiting for transfers between devices, carried_in(): everything = jax.tree.map(lambda part: lax.all_gather(part, axis), x)  190 us
    psum x1, waiting for transfers between devices, broadcast(): return lax.psum(jnp.where(mine, x, jnp.zeros_like(x)), axis)  85.2 us
    dot_general x27, matrix products, pair_combine(): jnp.einsum('...ij,...jk->...ik', late_move, early_rest, precision=exact_a...  51.5 us
    dot_general x19, matrix products, pair_combine(): jnp.einsum('...ij,...jk->...ik', late_move, early_move, precision=exact_a...  31.9 us
  transfers between devices with their start and end apart: 7, of which 7 were waited for; matrix products, arithmetic and copies ran while one was open for 3% of the time, Pallas kernels for 0%

commit v1 on v0

v1 whole, which is shorter than its diff:
```python
import functools

import jax
import jax.numpy as jnp
from jax import lax
from jax.experimental import pallas as pl
from jax.experimental.pallas import tpu as pltpu
from jax.sharding import PartitionSpec as P

HEADS = 8
HEAD = 128
WIDTH = 1024
ROWS = 512
PATCHES = 128
CHUNK = 128
CHUNKS = ROWS // CHUNK
PAIR = 2 * HEAD
RIM = 16
HALF = HEAD // 2
SLOT = HEAD + HALF
EPS = 1e-6
MESH = pl.DeviceIdType.MESH
F32 = jnp.float32
BF16 = jnp.bfloat16


def mm(a, b):
    return jnp.dot(a.astype(BF16), b.astype(BF16), preferred_element_type=F32)


def mm_nt(a, b):
    return lax.dot_general(
        a.astype(BF16), b.astype(BF16), (((1,), (1,)), ((), ())), preferred_element_type=F32
    )


def silu(v):
    return 0.5 * v * (1.0 + jnp.tanh(0.5 * v))


def grid_of(shape):
    return lax.broadcasted_iota(jnp.int32, shape, 0), lax.broadcasted_iota(jnp.int32, shape, 1)


def level_mask(rows, cols, block):
    same = rows // (2 * block) == cols // (2 * block)
    return same & ((rows // block) % 2 == 1) & ((cols // block) % 2 == 0)


def unit_lower_inverses(lowers):
    rows, cols = grid_of((CHUNK, CHUNK))
    eye = (rows == cols).astype(F32)
    first = level_mask(rows, cols, 1)
    solved = [(eye - jnp.where(first, low, 0.0)) for low in lowers]
    block = 2
    while block < CHUNK:
        mask = level_mask(rows, cols, block)
        halves = [mm(x, jnp.where(mask, low, 0.0)) for x, low in zip(solved, lowers)]
        solved = [x - mm(half, x) for half, x in zip(halves, solved)]
        block *= 2
    return solved


def prepare_kernel(
    bytes_ref, patches_ref, rim_ref, starts_ref, codes_ref, wq_ref, wk_ref, wv_ref,
    tq_ref, tk_ref, tv_ref, move_ref, qe_ref, oe_ref, hidden, extended,
):
    pair = pl.program_id(0)

    @pl.when(pair == 0)
    def _():
        place = lax.axis_index(("outer", "inner"))
        starts = starts_ref[...]
        rows, cols = grid_of((ROWS, PATCHES))
        positions = rows + place * ROWS
        following = jnp.where(
            cols == PATCHES - 1, jnp.int32(1 << 30), pltpu.roll(jnp.broadcast_to(starts, (ROWS, PATCHES)), PATCHES - 1, 1)
        )
        chosen = (positions >= starts) & (positions < following)
        picked = mm(chosen.astype(F32), patches_ref[...])
        before = positions[:, :1] < starts[:, :1]
        picked = jnp.where(before, rim_ref[RIM - 4 : RIM - 3, :].astype(F32), picked)
        hidden[RIM:, :] = (bytes_ref[...].astype(F32) + picked).astype(BF16)
        hidden[:RIM, :] = rim_ref[...]

    def activate(w_ref, taps_ref):
        projected = jnp.dot(hidden[...], w_ref[...], preferred_element_type=F32)
        extended[...] = projected.astype(BF16).astype(F32)
        running = taps_ref[0:1, :] * extended[RIM - 3 : RIM - 3 + ROWS, :]
        for tap in range(1, 4):
            running += taps_ref[tap : tap + 1, :] * extended[RIM - 3 + tap : RIM - 3 + tap + ROWS, :]
        return silu(running)

    queries = activate(wq_ref, tq_ref)
    keys = activate(wk_ref, tk_ref)
    values = activate(wv_ref, tv_ref)
    beta_all = codes_ref[...].astype(F32) * 0.25
    rows, cols = grid_of((CHUNK, CHUNK))
    lane = lax.broadcasted_iota(jnp.int32, (ROWS, HEADS), 1)
    items = []
    for half in range(2):
        span = slice(half * HEAD, (half + 1) * HEAD)
        k = keys[:, span]
        k = k * lax.rsqrt(jnp.sum(k * k, axis=1, keepdims=True) + EPS)
        beta = jnp.sum(jnp.where(lane == 2 * pair + half, beta_all, 0.0), axis=1, keepdims=True)
        for c in range(CHUNKS):
            part = slice(c * CHUNK, (c + 1) * CHUNK)
            items.append((queries[part, span].astype(BF16), k[part], values[part, span], beta[part]))
    grams = [mm_nt(k, k) for _, k, _, _ in items]
    scores = [jnp.where(rows >= cols, mm_nt(q, k), 0.0) for q, k, _, _ in items]
    lowers = [jnp.where(rows > cols, beta * gram, 0.0) for gram, (_, _, _, beta) in zip(grams, items)]
    inverses = unit_lower_inverses(lowers)
    solved = [
        mm(x, jnp.concatenate([-beta * k, beta * v], axis=1))
        for x, (_, k, v, beta) in zip(inverses, items)
    ]
    turned = [k.T.astype(BF16) for _, k, _, _ in items]
    for half in range(2):
        state = None
        for c in range(CHUNKS):
            at = half * CHUNKS + c
            q = items[at][0]
            minus_w_u = solved[at]
            if state is None:
                fresh = minus_w_u
                result = mm(scores[at], fresh)
                state = mm(turned[at], fresh)
            else:
                fresh = minus_w_u + mm(minus_w_u[:, :HEAD], state)
                result = mm(
                    jnp.concatenate([q, scores[at].astype(BF16)], axis=1),
                    jnp.concatenate([state.astype(BF16), fresh.astype(BF16)], axis=0),
                )
                state = state + mm(turned[at], fresh)
            part = slice(c * CHUNK, (c + 1) * CHUNK)
            span = slice(half * HEAD, (half + 1) * HEAD)
            qe_ref[part, span] = (result[:, :HEAD] + q.astype(F32)).astype(BF16)
            oe_ref[part, span] = result[:, HEAD:]
        move_t = state[:, :HEAD].T
        rest_t = state[:, HEAD:].T
        move_ref[half, :HALF, :] = rest_t[:HALF].astype(BF16)
        move_ref[half, HALF : HALF + HEAD, :] = move_t.astype(BF16)
        move_ref[half, HALF + HEAD :, :] = rest_t[HALF:].astype(BF16)


def prepare(byte_states, patch_vectors, rim, patch_starts, beta_codes, w_qkv, conv_taps):
    whole = lambda *shape: pl.BlockSpec(shape, lambda p: (0,) * len(shape))
    weight = lambda part: pl.BlockSpec((WIDTH, PAIR), lambda p: (0, 4 * part + p))
    taps = lambda part: pl.BlockSpec((4, PAIR), lambda p: (0, 4 * part + p))
    return pl.pallas_call(
        prepare_kernel,
        grid=(HEADS // 2,),
        in_specs=[
            whole(ROWS, WIDTH), whole(PATCHES, WIDTH), whole(RIM, WIDTH), whole(1, PATCHES), whole(ROWS, HEADS),
            weight(0), weight(1), weight(2), taps(0), taps(1), taps(2),
        ],
        out_specs=[
            pl.BlockSpec((2, 2 * HEAD, HEAD), lambda p: (p, 0, 0)),
            pl.BlockSpec((ROWS, PAIR), lambda p: (0, p)),
            pl.BlockSpec((ROWS, PAIR), lambda p: (0, p)),
        ],
        out_shape=[
            jax.ShapeDtypeStruct((HEADS, 2 * HEAD, HEAD), BF16),
            jax.ShapeDtypeStruct((ROWS, WIDTH), BF16),
            jax.ShapeDtypeStruct((ROWS, WIDTH), F32),
        ],
        scratch_shapes=[pltpu.VMEM((RIM + ROWS, WIDTH), BF16), pltpu.VMEM((RIM + ROWS, PAIR), F32)],
        compiler_params=pltpu.CompilerParams(vmem_limit_bytes=48 << 20),
    )(byte_states, patch_vectors, rim, patch_starts, beta_codes, w_qkv, w_qkv, w_qkv, conv_taps, conv_taps, conv_taps)


def carry_kernel(
    outer_count, inner_count, move_ref, out_ref, slots, before, total, totals, states, landed,
    sem_a, recv_a, sem_b, recv_b, sem_c, recv_c,
):
    outer = lax.axis_index("outer")
    inner = lax.axis_index("inner")
    barrier = pltpu.get_barrier_semaphore()
    for step in range(1, inner_count):
        peer = lax.rem(inner + step, inner_count)
        pl.semaphore_signal(barrier, inc=1, device_id=(outer, peer), device_id_type=MESH)
    for step in range(1, outer_count):
        peer = lax.rem(outer + step, outer_count)
        pl.semaphore_signal(barrier, inc=1, device_id=(peer, inner), device_id_type=MESH)
    pl.semaphore_wait(barrier, inner_count + outer_count - 2)

    def spread(step):
        peer = lax.rem(inner + step, inner_count)
        return pltpu.make_async_remote_copy(
            src_ref=move_ref.at[peer // 2, pl.ds(pl.multiple_of((peer % 2) * HALF, HALF), SLOT)],
            dst_ref=slots.at[inner],
            send_sem=sem_a.at[peer],
            recv_sem=recv_a.at[inner],
            device_id=(outer, peer),
            device_id_type=MESH,
        )

    def spread_from(source):
        return pltpu.make_async_remote_copy(
            src_ref=slots.at[source],
            dst_ref=slots.at[source],
            send_sem=sem_a.at[source],
            recv_sem=recv_a.at[source],
            device_id=(outer, source),
            device_id_type=MESH,
        )

    for step in range(1, inner_count):
        spread(step).start()
    half = inner % 2
    slots[inner] = move_ref[inner // 2, pl.ds(pl.multiple_of(half * HALF, HALF), SLOT), :]
    moves_at = pl.multiple_of((1 - half) * HALF, HALF)
    rests_at = pl.multiple_of(half * HEAD, HALF)

    def advance(source, x):
        @pl.when(source != inner)
        def _():
            spread_from(source).wait_recv()

        before[source] = x.astype(BF16)
        moved = mm(x, slots[source, pl.ds(moves_at, HEAD), :])
        return x + moved + slots[source].astype(F32)

    x = lax.fori_loop(0, inner_count, advance, jnp.zeros((SLOT, HEAD), F32))
    total[...] = x.astype(BF16)

    def outward(peer):
        return pltpu.make_async_remote_copy(
            src_ref=total,
            dst_ref=totals.at[outer],
            send_sem=sem_b.at[peer],
            recv_sem=recv_b.at[outer],
            device_id=(peer, inner),
            device_id_type=MESH,
        )

    def outward_from(source):
        return pltpu.make_async_remote_copy(
            src_ref=total,
            dst_ref=totals.at[source],
            send_sem=sem_b.at[source],
            recv_sem=recv_b.at[source],
            device_id=(source, inner),
            device_id_type=MESH,
        )

    for step in range(1, outer_count):
        peer = outer + step

        @pl.when(peer < outer_count)
        def _():
            outward(peer).start()

    def descend(source, s):
        outward_from(source).wait_recv()
        moved = mm(s, totals[source, pl.ds(moves_at, HEAD), :])
        return s + moved + totals[source, pl.ds(rests_at, HALF), :].astype(F32)

    s = lax.fori_loop(0, outer, descend, jnp.zeros((HALF, HEAD), F32))

    def give(peer):
        return pltpu.make_async_remote_copy(
            src_ref=states.at[peer],
            dst_ref=landed.at[inner],
            send_sem=sem_c.at[peer],
            recv_sem=recv_c.at[inner],
            device_id=(outer, peer),
            device_id_type=MESH,
        )

    def give_from(source):
        return pltpu.make_async_remote_copy(
            src_ref=states.at[source],
            dst_ref=landed.at[source],
            send_sem=sem_c.at[source],
            recv_sem=recv_c.at[source],
            device_id=(outer, source),
            device_id_type=MESH,
        )

    for step in range(inner_count):
        peer = lax.rem(inner + step, inner_count)
        moved = mm(s, before[peer, pl.ds(moves_at, HEAD), :])
        at_start = s + moved + before[peer, pl.ds(rests_at, HALF), :].astype(F32)
        if step == 0:
            landed[inner] = at_start.astype(BF16)
        else:
            states[peer] = at_start.astype(BF16)
            give(peer).start()
    for step in range(1, inner_count):
        source = lax.rem(inner + step, inner_count)
        give_from(source).wait_recv()
    out_ref[...] = landed[...]
    for step in range(1, inner_count):
        peer = lax.rem(inner + step, inner_count)
        spread_from(peer).wait_send()
        give_from(peer).wait_send()
    for step in range(1, outer_count):
        peer = outer + step

        @pl.when(peer < outer_count)
        def _():
            outward(peer).wait_send()


def carry(move, outer_count, inner_count):
    dma = lambda n: pltpu.SemaphoreType.DMA((n,))
    return pl.pallas_call(
        functools.partial(carry_kernel, outer_count, inner_count),
        in_specs=[pl.BlockSpec(memory_space=pltpu.VMEM)],
        out_specs=pl.BlockSpec(memory_space=pltpu.VMEM),
        out_shape=jax.ShapeDtypeStruct((2 * HEADS, HALF, HEAD), BF16),
        scratch_shapes=[
            pltpu.VMEM((inner_count, SLOT, HEAD), BF16),
            pltpu.VMEM((inner_count, SLOT, HEAD), BF16),
            pltpu.VMEM((SLOT, HEAD), BF16),
            pltpu.VMEM((outer_count, SLOT, HEAD), BF16),
            pltpu.VMEM((inner_count, HALF, HEAD), BF16),
            pltpu.VMEM((2 * HEADS, HALF, HEAD), BF16),
            dma(inner_count), dma(inner_count), dma(outer_count), dma(outer_count), dma(inner_count), dma(inner_count),
        ],
        compiler_params=pltpu.CompilerParams(
            collective_id=0, has_side_effects=True, vmem_limit_bytes=32 << 20
        ),
    )(move)


def finish_kernel(qe_ref, oe_ref, states_ref, gain_ref, w_ref, out_ref):
    parts = []
    for head in range(HEADS):
        span = slice(head * HEAD, (head + 1) * HEAD)
        state = jnp.concatenate([states_ref[2 * head], states_ref[2 * head + 1]], axis=0)
        out = oe_ref[:, span] + mm_nt(qe_ref[:, span], state)
        mean = jnp.sum(out * out, axis=1, keepdims=True) * (1.0 / HEAD)
        parts.append((out * lax.rsqrt(mean + EPS) * gain_ref[:, span]).astype(BF16))
    normed = jnp.concatenate(parts, axis=1)
    out_ref[...] = jnp.dot(normed, w_ref[...], preferred_element_type=F32).astype(BF16)


def finish(qe, oe, states, gain, w_out):
    tile = 128
    whole = lambda *shape: pl.BlockSpec(shape, lambda p: (0,) * len(shape))
    return pl.pallas_call(
        finish_kernel,
        grid=(ROWS // tile,),
        in_specs=[
            pl.BlockSpec((tile, WIDTH), lambda p: (p, 0)),
            pl.BlockSpec((tile, WIDTH), lambda p: (p, 0)),
            whole(2 * HEADS, HALF, HEAD), whole(1, WIDTH), whole(WIDTH, WIDTH),
        ],
        out_specs=pl.BlockSpec((tile, WIDTH), lambda p: (p, 0)),
        out_shape=jax.ShapeDtypeStruct((ROWS, WIDTH), BF16),
        compiler_params=pltpu.CompilerParams(vmem_limit_bytes=32 << 20),
    )(qe, oe, states, gain, w_out)


def shifted(value, axis, steps):
    count = lax.axis_size(axis)
    return lax.ppermute(value, axis, [(source, source + steps) for source in range(count - steps)])


def local(byte_states, patch_vectors, patch_starts, beta_codes, w_qkv, conv_taps, norm_gain, w_out):
    place = lax.axis_index(("outer", "inner"))
    last = jnp.arange(ROWS - 3, ROWS, dtype=jnp.int32) + place * ROWS
    index = jnp.sum((patch_starts[None, :] <= last[:, None]).astype(jnp.int32), axis=1) - 1
    fetched = jnp.take(patch_vectors, index, axis=0)
    rim = (byte_states[ROWS - 3 :].astype(F32) + fetched.astype(F32)).astype(BF16)
    rim = jnp.concatenate([jnp.zeros((RIM - 4, WIDTH), BF16), patch_vectors[PATCHES - 1 :], rim], axis=0)
    rim = shifted(rim, ("outer", "inner"), 1)
    move, qe, oe = prepare(
        byte_states, patch_vectors, rim, patch_starts.reshape(1, PATCHES), beta_codes, w_qkv, conv_taps
    )
    states = carry(move, lax.axis_size("outer"), lax.axis_size("inner"))
    return finish(qe, oe, states, norm_gain.reshape(1, WIDTH), w_out)


def solution(mesh):
    in_specs = (
        P(("outer", "inner"), None),
        P(("outer", "inner"), None),
        P(("outer", "inner")),
        P(("outer", "inner"), None),
        P(),
        P(),
        P(),
        P(),
    )
    out_specs = P(("outer", "inner"), None)
    return jax.shard_map(local, mesh=mesh, in_specs=in_specs, out_specs=out_specs, check_vma=False)
```

time: 539 us -> 76.4 us (0.14); the launches traced: 530 us -> 75.7 us
  waiting for transfers between devices: 285 us -> 6.04 us
  matrix products: 178 us -> 0 us
  Pallas kernels: 0 us -> 58 us
  local copies, waits for them, and re-layouts: 27.1 us -> 6.76 us
  other arithmetic: 18.6 us -> 1.73 us
  between operations: 14.3 us -> 0.08 us
    all_gather x4 -> x0, waiting for transfers between devices: 190 us -> none  [carried_in(): everything = jax.tree.map(lambda part: lax.all_gather(part, axis), x)]
    dot_general x132 -> x0, matrix products: 178 us -> none  [the longest x27 51.5 us: pair_combine(): jnp.einsum('...ij,...jk->...ik', late_move, early_rest, precision=exact_a...]
    psum x1 -> x0, waiting for transfers between devices: 85.2 us -> none  [broadcast(): return lax.psum(jnp.where(mine, x, jnp.zeros_like(x)), axis)]
    pallas_call x0 -> x3, Pallas kernels: none -> 58 us  [the longest x1 28.7 us: carry(): pl.pallas_call(functools.partial(carry_kernel, outer_count, inner_count),...]
    slice x7 -> x1, local copies, waits for them, and re-layouts: 10.3 us -> 0.73 us  [local(): patch_vectors[PATCHES - 1:]]
  transfers between devices with their start and end apart: 7 -> 1, of which waited for: 7 -> 1; matrix products, arithmetic and copies ran while one was open for 3% -> 1% of each run, Pallas kernels for 0% -> 0%
where the time goes in v1:
time: 76.4 us; the launch traced here: 75.7 us
  Pallas kernels  58 us (76%)
  local copies, waits for them, and re-layouts  6.76 us (9%)
  waiting for transfers between devices  6.04 us (8%)
  starting transfers between devices  3.11 us (4%)
  other arithmetic  1.73 us (2%)
    pallas_call x1, Pallas kernels, carry(): pl.pallas_call(functools.partial(carry_kernel, outer_count, inner_count),...  28.7 us
    pallas_call x1, Pallas kernels, prepare(): pl.pallas_call(prepare_kernel, grid=(HEADS // 2,), in_specs=[whole(ROWS,...  25.7 us
    ppermute x1, waiting for transfers between devices, shifted(): lax.ppermute(value, axis, [(source, source + steps) for source in range(c...  6.04 us
    unnamed x13, local copies, waits for them, and re-layouts  4.47 us
    pallas_call x1, Pallas kernels, finish(): pl.pallas_call(finish_kernel, grid=(ROWS // tile,), in_specs=[pl.BlockSpe...  3.62 us
    ppermute x1, starting transfers between devices, shifted(): lax.ppermute(value, axis, [(source, source + steps) for source in range(c...  3.11 us
    gather x1, local copies, waits for them, and re-layouts, local(): fetched = jnp.take(patch_vectors, index, axis=0)  1.55 us
  transfers between devices with their start and end apart: 1, of which 1 were waited for; matrix products, arithmetic and copies ran while one was open for 1% of the time, Pallas kernels for 0%

profile of v1, /device:TPU:17, one launch (start us, length us, event | category | flops | bytes accessed | tf_op | source)
XLA Modules:
  0.0 75.7 jit_solution(9453735311097038485)
XLA Ops:
  0.0 0.8 %convert_reduce_fusion = s32[3]{0:T(128)S(1)} fusion(s32[128]{0:T(128)} %param.10, s32[3]{0:T(128)S(1)} %add_add_fusion), kind=kLoop, calls=%fused_computation.6 | loop fusion | flops 1149 | bytes 536 | tf_op jit(solution)/shard_map/reduce_sum | solution.py:365
  0.9 0.7 slice.6
  1.6 1.6 %gather_fusion = bf16[3,1024]{1,0:T(4,128)(2,1)S(1)} fusion(bf16[128,1024]{1,0:T(8,128)(2,1)} %patches_ref.1, s32[1024]{0:T(1024)S(1)} %pad_clamp_fusion), kind=kCustom, calls=%fused_computation | custom fusion | bytes 12300 | tf_op jit(solution)/shard_map/jit(_take)/gather | solution.py:366
  3.2 0.8 %add_convert_fusion = bf16[3,1024]{1,0:T(4,128)(2,1)S(1)} fusion(bf16[3,1024]{1,0:T(4,128)(2,1)S(1)} %gather_fusion, bf16[512,1024]{1,0:T(8,128)(2,1)} %bytes_ref.1, pred[3]{0:T(512)(128)(4,1)S(1)} %compare_and_fusion), kind=kLoop, calls=%fused_computation.2 | loop fusion | flops 15360 | bytes 18435 | tf_op jit(solution)/shard_map/convert_element_type | solution.py:367
  4.0 0.1 pad_maximum_fusion
  4.1 3.1 %collective-permute-start = (bf16[16,1024]{1,0:T(8,128)(2,1)S(1)}, bf16[16,1024]{1,0:T(8,128)(2,1)S(1)}, u32[]{:S(2)}, u32[]{:S(2)}) collective-permute-start(bf16[16,1024]{1,0:T(8,128)(2,1)S(1)} %pad_maximum_fusion), channel_id=1, source_target_pairs={{0,1},{1,2},{2,3},{3,4},{4,5},{5,6},{6,7},{7,8},{8,9},{9,10},{10,1... | collective-permute-start | bytes 98312 | tf_op jit(solution)/shard_map/ppermute | solution.py:359
  7.2 0.8 %copy.10.codes_ref = s32[512,8]{1,0:T(8,128)S(1)} copy(s32[512,8]{0,1:T(8,128)} %param.11) | data formatting | bytes 32768 | tf_op args[3]
  8.0 6.0 %collective-permute-done.rim_ref = bf16[16,1024]{1,0:T(8,128)(2,1)S(1)} collective-permute-done((bf16[16,1024]{1,0:T(8,128)(2,1)S(1)}, bf16[16,1024]{1,0:T(8,128)(2,1)S(1)}, u32[]{:S(2)}, u32[]{:S(2)}) %collective-permute-start) | collective-permute-done | bytes 32800 | tf_op jit(solution)/shard_map/ppermute | solution.py:359
  14.1 0.0 copy-start.1
  14.1 1.2 %copy-done.1 = bf16[512,1024]{1,0:T(8,128)(2,1)S(1)} copy-done((bf16[512,1024]{1,0:T(8,128)(2,1)S(1)}, bf16[512,1024]{1,0:T(8,128)(2,1)}, u32[]{:S(2)}) %copy-start.1) | copy-done | bytes 1048600
  15.3 0.0 copy-start.2
  15.3 0.8 %copy-done.2 = f32[4,3072]{1,0:T(4,128)S(1)} copy-done((f32[4,3072]{1,0:T(4,128)S(1)}, f32[4,3072]{1,0:T(4,128)}, u32[]{:S(2)}) %copy-start.2) | copy-done | bytes 49176
  16.1 0.0 copy-start.3
  16.1 0.9 %copy-done.3 = bf16[128,1024]{1,0:T(8,128)(2,1)S(1)} copy-done((bf16[128,1024]{1,0:T(8,128)(2,1)S(1)}, bf16[128,1024]{1,0:T(8,128)(2,1)}, u32[]{:S(2)}) %copy-start.3) | copy-done | bytes 262168
  17.0 0.0 copy-start.5
  17.0 0.7 copy-done.5
  17.7 0.0 copy-start
  17.7 0.0 copy-start.4
  17.7 25.7 %shard_map.82 = (bf16[8,256,128]{2,1,0:T(8,128)(2,1)S(1)}, bf16[512,1024]{1,0:T(8,128)(2,1)S(1)}, f32[512,1024]{1,0:T(8,128)S(1)}) custom-call(bf16[512,1024]{1,0:T(8,128)(2,1)S(1)} %copy-done.1, bf16[128,1024]{1,0:T(8,128)(2,1)S(1)} %copy-done.3, bf16[16,1024]{1,0:T(8,128)(2,1)S(1)} %collective-permute-done.rim_ref, s32[1,128]{1,0:T(1,128)S(1)} %bitcast.9, ...), custom_call_target="tpu_custom_call" | custom-call | tf_op jit(solution)/shard_map/pallas_call | solution.py:150
  43.4 28.7 %shard_map.83.states_ref = bf16[16,64,128]{2,1,0:T(8,128)(2,1)S(1)} custom-call(bf16[8,256,128]{2,1,0:T(8,128)(2,1)S(1)} %get-tuple-element.10.move_ref), custom_call_target="tpu_custom_call" | custom-call | tf_op jit(solution)/shard_map/pallas_call | solution.py:308
  72.1 0.0 copy-done
  72.1 0.0 copy-done.4
  72.1 3.6 %shard_map.84 = bf16[512,1024]{1,0:T(8,128)(2,1)} custom-call(bf16[512,1024]{1,0:T(8,128)(2,1)S(1)} %get-tuple-element.8.qe_ref, f32[512,1024]{1,0:T(8,128)S(1)} %get-tuple-element.9.oe_ref, bf16[16,64,128]{2,1,0:T(8,128)(2,1)S(1)} %shard_map.83.states_ref, f32[1,1024]{1,0:T(1,128)S(1)} %bitcast.8, bf16[1024,1024]{1,0:T(8,128)(2,1)S(1)} %copy-done), custom_call_target="tpu_custom_call" | custom-call | tf_op jit(solution)/shard_map/pallas_call | solution.py:343
  (6 shorter events, 0.0 us)
Async XLA Ops:
  4.1 10.0 %collective-permute-start = (bf16[16,1024]{1,0:T(8,128)(2,1)S(1)}, bf16[16,1024]{1,0:T(8,128)(2,1)S(1)}, u32[]{:S(2)}, u32[]{:S(2)}) collective-permute-start(bf16[16,1024]{1,0:T(8,128)(2,1)S(1)} %pad_maximum_fusion), channel_id=1, source_target_pairs={{0,1},{1,2},{2,3},{3,4},{4,5},{5,6},{6,7},{7,8},{8,9},{9,10},{10,1... | collective-permute-start | bytes 98312 | tf_op jit(solution)/shard_map/ppermute | solution.py:359
  14.1 1.2 %copy-start.1 = (bf16[512,1024]{1,0:T(8,128)(2,1)S(1)}, bf16[512,1024]{1,0:T(8,128)(2,1)}, u32[]{:S(2)}) copy-start(bf16[512,1024]{1,0:T(8,128)(2,1)} %bytes_ref.1) | copy-start | bytes 3145732
  15.3 0.8 %copy-start.2 = (f32[4,3072]{1,0:T(4,128)S(1)}, f32[4,3072]{1,0:T(4,128)}, u32[]{:S(2)}) copy-start(f32[4,3072]{1,0:T(4,128)} %tv_ref.1) | copy-start | bytes 147460
  16.1 0.9 %copy-start.3 = (bf16[128,1024]{1,0:T(8,128)(2,1)S(1)}, bf16[128,1024]{1,0:T(8,128)(2,1)}, u32[]{:S(2)}) copy-start(bf16[128,1024]{1,0:T(8,128)(2,1)} %patches_ref.1) | copy-start | bytes 786436
  17.0 0.7 copy-start.5
  17.7 54.4 %copy-start = (bf16[1024,1024]{1,0:T(8,128)(2,1)S(1)}, bf16[1024,1024]{1,0:T(8,128)(2,1)}, u32[]{:S(2)}) copy-start(bf16[1024,1024]{1,0:T(8,128)(2,1)} %w_ref.1) | copy-start | bytes 6291460
  17.7 54.4 %copy-start.4 = (f32[1024]{0:T(1024)S(1)}, f32[1024]{0:T(1024)}, u32[]{:S(2)}) copy-start(f32[1024]{0:T(1024)} %param.14) | copy-start | bytes 12292

commit v2 on v1

v2 whole, which is shorter than its diff:
```python
import functools

import jax
import jax.numpy as jnp
from jax import lax
from jax.experimental import pallas as pl
from jax.experimental.pallas import tpu as pltpu
from jax.sharding import PartitionSpec as P

HEADS = 8
HEAD = 128
WIDTH = 1024
ROWS = 512
PATCHES = 128
CHUNK = 128
RIM = 16
HALF_ROWS = ROWS // 2
GROUP = HEADS // 2
COLS = GROUP * HEAD
HALF = HEAD // 2
SLOT = HEAD + HALF
EPS = 1e-6
MESH = pl.DeviceIdType.MESH
F32 = jnp.float32
BF16 = jnp.bfloat16


def mm(a, b):
    return jnp.dot(a.astype(BF16), b.astype(BF16), preferred_element_type=F32)


def mm_nt(a, b):
    return lax.dot_general(
        a.astype(BF16), b.astype(BF16), (((1,), (1,)), ((), ())), preferred_element_type=F32
    )


def silu(v):
    return 0.5 * v * (1.0 + jnp.tanh(0.5 * v))


def grid_of(shape):
    return lax.broadcasted_iota(jnp.int32, shape, 0), lax.broadcasted_iota(jnp.int32, shape, 1)


def level_mask(rows, cols, block):
    same = rows // (2 * block) == cols // (2 * block)
    return same & ((rows // block) % 2 == 1) & ((cols // block) % 2 == 0)


def unit_lower_inverses(lowers):
    rows, cols = grid_of((CHUNK, CHUNK))
    eye = (rows == cols).astype(F32)
    first = level_mask(rows, cols, 1)
    solved = [(eye - jnp.where(first, low, 0.0)) for low in lowers]
    block = 2
    while block < CHUNK:
        mask = level_mask(rows, cols, block)
        halves = [mm(x, jnp.where(mask, low, 0.0)) for x, low in zip(solved, lowers)]
        solved = [x - mm(half, x) for half, x in zip(halves, solved)]
        block *= 2
    return solved


def joined(earlier, later):
    return earlier + later + mm(earlier, later[:HEAD])


def kernel(
    outer_count, inner_count,
    bytes_hbm, patches_hbm, starts_ref, codes_ref, w_hbm, taps_ref, gain_ref, wout_hbm, out_ref,
    hidden, patches, weights, wout, rim_out, rim_in, betas, ext_k, ext_v, ext_q, unit_keys, solved_ref,
    firsts, pairs, moves, slots, before, tree, total, totals, states, landed, qe, oe,
    sem_in, sem_rim, sem_a, recv_a, sem_b, recv_b, sem_c, recv_c,
):
    outer = lax.axis_index("outer")
    inner = lax.axis_index("inner")
    place = outer * inner_count + inner
    devices = outer_count * inner_count

    loads = [
        pltpu.make_async_copy(bytes_hbm, hidden.at[pl.ds(RIM, ROWS)], sem_in.at[0]),
        pltpu.make_async_copy(patches_hbm, patches, sem_in.at[1]),
    ]
    for at, (part, group) in enumerate([(1, 0), (2, 0), (1, 1), (2, 1), (0, 0), (0, 1)]):
        loads.append(
            pltpu.make_async_copy(
                w_hbm.at[:, pl.ds(part * WIDTH + group * COLS, COLS)], weights.at[part, group], sem_in.at[2 + at]
            )
        )
    loads.append(pltpu.make_async_copy(wout_hbm, wout, sem_in.at[8]))
    for load in loads:
        load.start()

    barrier = pltpu.get_barrier_semaphore()

    def device_at(index):
        index = lax.rem(index + devices, devices)
        return (index // inner_count, lax.rem(index, inner_count))

    following, preceding = device_at(place + 1), device_at(place - 1)
    for neighbour in (following, preceding):
        pl.semaphore_signal(barrier, inc=1, device_id=neighbour, device_id_type=MESH)
    for step in range(1, inner_count):
        peer = lax.rem(inner + step, inner_count)
        pl.semaphore_signal(barrier, inc=1, device_id=(outer, peer), device_id_type=MESH)
    for step in range(1, outer_count):
        peer = lax.rem(outer + step, outer_count)
        pl.semaphore_signal(barrier, inc=1, device_id=(peer, inner), device_id_type=MESH)

    starts = starts_ref[...]
    rows, cols = grid_of((ROWS, PATCHES))
    positions = rows + place * ROWS
    next_starts = jnp.where(cols == PATCHES - 1, jnp.int32(1 << 30), pltpu.roll(jnp.broadcast_to(starts, (ROWS, PATCHES)), PATCHES - 1, 1))
    chosen = ((positions >= starts) & (positions < next_starts)).astype(BF16)
    open_rows = positions[:, :1] < starts[:, :1]
    for group in range(2):
        turned = codes_ref[group * GROUP : (group + 1) * GROUP, :].astype(F32) * 0.25
        betas[group] = turned.T
    loads[0].wait()
    loads[1].wait()
    picked = jnp.dot(chosen, patches[...], preferred_element_type=F32)
    hidden[RIM:, :] = (hidden[RIM:, :].astype(F32) + picked).astype(BF16)
    rim_rows, _ = grid_of((RIM, WIDTH))
    rim_out[...] = jnp.where(
        rim_rows == RIM - 4, patches[PATCHES - 1 :, :].astype(F32), hidden[ROWS:, :].astype(F32)
    ).astype(BF16)
    pl.semaphore_wait(barrier, inner_count + outer_count)
    rim_copy = pltpu.make_async_remote_copy(
        src_ref=rim_out, dst_ref=rim_in, send_sem=sem_rim.at[0], recv_sem=sem_rim.at[1],
        device_id=following, device_id_type=MESH,
    )
    rim_copy.start()
    for load in loads[2:6]:
        load.wait()
    rim_copy.wait_recv()
    rim = jnp.where(place > 0, rim_in[...].astype(F32), 0.0)
    hidden[:RIM, :] = rim.astype(BF16)
    filled = hidden[RIM:, :].astype(F32)
    hidden[RIM:, :] = jnp.where(open_rows, filled + rim[RIM - 4 : RIM - 3, :], filled).astype(BF16)

    def activate(part, row_half, group, ext):
        here = hidden[pl.ds(pl.multiple_of(row_half * HALF_ROWS, HALF_ROWS), HALF_ROWS + RIM), :]
        projected = jnp.dot(here, weights[part, group], preferred_element_type=F32)
        ext[...] = projected.astype(BF16).astype(F32)
        lanes = pl.ds(pl.multiple_of(part * WIDTH + group * COLS, COLS), COLS)
        running = taps_ref[0:1, lanes] * ext[RIM - 3 : RIM - 3 + HALF_ROWS, :]
        for tap in range(1, 4):
            running += taps_ref[tap : tap + 1, lanes] * ext[RIM - 3 + tap : RIM - 3 + tap + HALF_ROWS, :]
        return silu(running)

    tile_rows, tile_cols = grid_of((CHUNK, CHUNK))

    def spread(role):
        return pltpu.make_async_remote_copy(
            src_ref=moves.at[role], dst_ref=slots.at[inner], send_sem=sem_a.at[role], recv_sem=recv_a.at[inner],
            device_id=(outer, role), device_id_type=MESH,
        )

    def spread_from(source):
        return pltpu.make_async_remote_copy(
            src_ref=moves.at[source], dst_ref=slots.at[source], send_sem=sem_a.at[source], recv_sem=recv_a.at[source],
            device_id=(outer, source), device_id_type=MESH,
        )

    def critical(step, _):
        row_half, group = 1 - step // 2, lax.rem(step, 2)
        keys = activate(1, row_half, group, ext_k)
        values = activate(2, row_half, group, ext_v)
        beta = betas[group, pl.ds(pl.multiple_of(row_half * HALF_ROWS, HALF_ROWS), HALF_ROWS), :]
        items = []
        for head in range(GROUP):
            span = slice(head * HEAD, (head + 1) * HEAD)
            k = keys[:, span]
            k = k * lax.rsqrt(jnp.sum(k * k, axis=1, keepdims=True) + EPS)
            unit_keys[row_half, group, head] = k.astype(BF16)
            for c in range(2):
                part = slice(c * CHUNK, (c + 1) * CHUNK)
                items.append((k[part], values[part, span], beta[part, head : head + 1]))
        lowers = [jnp.where(tile_rows > tile_cols, beta * mm_nt(k, k), 0.0) for k, _, beta in items]
        inverses = unit_lower_inverses(lowers)
        solved = [
            mm(x, jnp.concatenate([-beta * k, beta * v], axis=1)).astype(BF16)
            for x, (k, v, beta) in zip(inverses, items)
        ]
        parts = [mm(k.T, s) for (k, _, _), s in zip(items, solved)]
        for head in range(GROUP):
            first, second = parts[2 * head], parts[2 * head + 1]
            for c in range(2):
                solved_ref[row_half, group, head, c] = solved[2 * head + c]
            firsts[row_half, group, head] = first.astype(BF16)
            pairs[row_half, group, head] = first + second + mm(second[:, :HEAD], first)

        @pl.when(row_half == 0)
        def _():
            for head in range(GROUP):
                early, late = pairs[0, group, head], pairs[1, group, head]
                whole = early + late + mm(late[:, :HEAD], early)
                move = whole[:, :HEAD].T.astype(BF16)
                rest = whole[:, HEAD:].T.astype(BF16)
                for half in range(2):
                    role = (group * GROUP + head) * 2 + half
                    moves[role, :HEAD, :] = move
                    moves[role, HEAD:, :] = rest[half * HALF : (half + 1) * HALF]

            for at in range(2 * GROUP):
                role = group * 2 * GROUP + at

                @pl.when(role != inner)
                def _():
                    spread(role).start()

                @pl.when(role == inner)
                def _():
                    slots[inner] = moves[role]

        return 0

    lax.fori_loop(0, 4, critical, 0)

    for load in loads[6:8]:
        load.wait()

    def deferred(step, _):
        row_half, group = step // 2, lax.rem(step, 2)
        queries = activate(0, row_half, group, ext_q)
        late = (row_half == 1).astype(F32)
        for head in range(GROUP):
            span = slice(head * HEAD, (head + 1) * HEAD)
            k = unit_keys[row_half, group, head]
            first = firsts[row_half, group, head]
            state_a = pairs[0, group, head] * late
            state_b = state_a + first.astype(F32) + mm(first[:, :HEAD], state_a)
            for c, state in enumerate((state_a, state_b)):
                part = slice(c * CHUNK, (c + 1) * CHUNK)
                q = queries[part, span]
                score = jnp.where(tile_rows >= tile_cols, mm_nt(q, k[part]), 0.0)
                base = mm(score, solved_ref[row_half, group, head, c])
                reach = base[:, :HEAD] + q
                result = mm(reach, state)
                to = pl.ds(pl.multiple_of(row_half * HALF_ROWS + c * CHUNK, CHUNK), CHUNK)
                qe[group, head, to, :] = (reach + result[:, :HEAD]).astype(BF16)
                oe[group, head, to, :] = base[:, HEAD:] + result[:, HEAD:]
        return 0

    lax.fori_loop(0, 4, deferred, 0)

    for step in range(1, inner_count):
        spread_from(lax.rem(inner + step, inner_count)).wait_recv()
    for at in range(inner_count // 2):
        tree[at] = joined(slots[2 * at].astype(F32), slots[2 * at + 1].astype(F32)).astype(BF16)
    count = inner_count // 4
    while count:
        for at in range(count):
            tree[at] = joined(tree[2 * at].astype(F32), tree[2 * at + 1].astype(F32)).astype(BF16)
        count //= 2
    total[...] = tree[0]

    def outward(peer):
        return pltpu.make_async_remote_copy(
            src_ref=total, dst_ref=totals.at[outer], send_sem=sem_b.at[peer], recv_sem=recv_b.at[outer],
            device_id=(peer, inner), device_id_type=MESH,
        )

    def outward_from(source):
        return pltpu.make_async_remote_copy(
            src_ref=total, dst_ref=totals.at[source], send_sem=sem_b.at[source], recv_sem=recv_b.at[source],
            device_id=(source, inner), device_id_type=MESH,
        )

    for step in range(1, outer_count):
        peer = outer + step

        @pl.when(peer < outer_count)
        def _():
            outward(peer).start()

    running = jnp.zeros((SLOT, HEAD), F32)
    for at in range(inner_count):
        before[at] = running.astype(BF16)
        if at < inner_count - 1:
            running = joined(running, slots[at].astype(F32))

    def descend(source, s):
        outward_from(source).wait_recv()
        return s + mm(s, totals[source, :HEAD, :]) + totals[source, HEAD:, :].astype(F32)

    s = lax.fori_loop(0, outer, descend, jnp.zeros((HALF, HEAD), F32))

    def give(peer):
        return pltpu.make_async_remote_copy(
            src_ref=states.at[peer], dst_ref=landed.at[inner], send_sem=sem_c.at[peer], recv_sem=recv_c.at[inner],
            device_id=(outer, peer), device_id_type=MESH,
        )

    def give_from(source):
        return pltpu.make_async_remote_copy(
            src_ref=states.at[source], dst_ref=landed.at[source], send_sem=sem_c.at[source],
            recv_sem=recv_c.at[source], device_id=(outer, source), device_id_type=MESH,
        )

    for step in range(1, inner_count + 1):
        peer = lax.rem(inner + step, inner_count)
        at_start = (s + mm(s, before[peer, :HEAD, :]) + before[peer, HEAD:, :].astype(F32)).astype(BF16)
        if step == inner_count:
            landed[inner] = at_start
        else:
            states[peer] = at_start
            give(peer).start()
    loads[8].wait()
    for step in range(1, inner_count):
        give_from(lax.rem(inner + step, inner_count)).wait_recv()

    def finish(tile, _):
        at = pl.ds(pl.multiple_of(tile * CHUNK, CHUNK), CHUNK)
        parts = []
        for head in range(HEADS):
            state = jnp.concatenate([landed[2 * head], landed[2 * head + 1]], axis=0)
            group, inside = head // GROUP, head % GROUP
            result = oe[group, inside, at, :] + mm_nt(qe[group, inside, at, :], state)
            mean = jnp.sum(result * result, axis=1, keepdims=True) * (1.0 / HEAD)
            gain = gain_ref[:, head * HEAD : (head + 1) * HEAD]
            parts.append((result * lax.rsqrt(mean + EPS) * gain).astype(BF16))
        normed = jnp.concatenate(parts, axis=1)
        out_ref[at, :] = jnp.dot(normed, wout[...], preferred_element_type=F32).astype(BF16)
        return 0

    lax.fori_loop(0, ROWS // CHUNK, finish, 0)

    rim_copy.wait_send()
    for step in range(1, inner_count):
        peer = lax.rem(inner + step, inner_count)
        spread_from(peer).wait_send()
        give_from(peer).wait_send()
    for step in range(1, outer_count):
        peer = outer + step

        @pl.when(peer < outer_count)
        def _():
            outward(peer).wait_send()


def local(byte_states, patch_vectors, patch_starts, beta_codes, w_qkv, conv_taps, norm_gain, w_out):
    outer_count, inner_count = lax.axis_size("outer"), lax.axis_size("inner")
    dma = lambda *n: pltpu.SemaphoreType.DMA(n)
    vmem = lambda *shape: pltpu.VMEM(shape, BF16)
    wide = lambda *shape: pltpu.VMEM(shape, F32)
    here, far = pl.BlockSpec(memory_space=pltpu.VMEM), pl.BlockSpec(memory_space=pl.ANY)
    return pl.pallas_call(
        functools.partial(kernel, outer_count, inner_count),
        in_specs=[far, far, here, here, far, here, here, far],
        out_specs=here,
        out_shape=jax.ShapeDtypeStruct((ROWS, WIDTH), BF16),
        scratch_shapes=[
            vmem(RIM + ROWS, WIDTH),
            vmem(PATCHES, WIDTH),
            vmem(3, 2, WIDTH, COLS),
            vmem(WIDTH, WIDTH),
            vmem(RIM, WIDTH),
            vmem(RIM, WIDTH),
            wide(2, ROWS, GROUP),
            wide(RIM + HALF_ROWS, COLS),
            wide(RIM + HALF_ROWS, COLS),
            wide(RIM + HALF_ROWS, COLS),
            vmem(2, 2, GROUP, HALF_ROWS, HEAD),
            vmem(2, 2, GROUP, 2, CHUNK, 2 * HEAD),
            vmem(2, 2, GROUP, HEAD, 2 * HEAD),
            wide(2, 2, GROUP, HEAD, 2 * HEAD),
            vmem(inner_count, SLOT, HEAD),
            vmem(inner_count, SLOT, HEAD),
            vmem(inner_count, SLOT, HEAD),
            vmem(inner_count // 2, SLOT, HEAD),
            vmem(SLOT, HEAD),
            vmem(outer_count, SLOT, HEAD),
            vmem(inner_count, HALF, HEAD),
            vmem(inner_count, HALF, HEAD),
            vmem(2, GROUP, ROWS, HEAD),
            wide(2, GROUP, ROWS, HEAD),
            dma(9), dma(2),
            dma(inner_count), dma(inner_count), dma(outer_count), dma(outer_count), dma(inner_count), dma(inner_count),
        ],
        compiler_params=pltpu.CompilerParams(
            collective_id=0, has_side_effects=True, vmem_limit_bytes=63 << 20
        ),
    )(
        byte_states, patch_vectors, patch_starts.reshape(1, PATCHES), beta_codes.T, w_qkv, conv_taps,
        norm_gain.reshape(1, WIDTH), w_out,
    )


def solution(mesh):
    in_specs = (
        P(("outer", "inner"), None),
        P(("outer", "inner"), None),
        P(("outer", "inner")),
        P(("outer", "inner"), None),
        P(),
        P(),
        P(),
        P(),
    )
    out_specs = P(("outer", "inner"), None)
    return jax.shard_map(local, mesh=mesh, in_specs=in_specs, out_specs=out_specs, check_vma=False)
```

time: 76.4 us -> 55.3 us (0.72)
  waiting for transfers between devices: 6.04 us -> 0 us
  Pallas kernels: 58 us -> 52.7 us
  local copies, waits for them, and re-layouts: 6.76 us -> 2.26 us
  starting transfers between devices: 3.11 us -> 0 us
  other arithmetic: 1.73 us -> 0 us
    ppermute x1 -> x0, waiting for transfers between devices: 6.04 us -> none  [shifted(): lax.ppermute(value, axis, [(source, source + steps) for source in range(c...]
    pallas_call x3 -> x1, Pallas kernels: 58 us -> 52.7 us  [local(): pl.pallas_call(functools.partial(kernel, outer_count, inner_count), in_sp...]
    ppermute x1 -> x0, starting transfers between devices: 3.11 us -> none  [shifted(): lax.ppermute(value, axis, [(source, source + steps) for source in range(c...]
    unnamed x13 -> x1, local copies, waits for them, and re-layouts: 4.47 us -> 2.26 us
    gather x1 -> x0, local copies, waits for them, and re-layouts: 1.55 us -> none  [local(): fetched = jnp.take(patch_vectors, index, axis=0)]
    reduce_sum x1 -> x0, other arithmetic: 0.84 us -> none  [local(): jnp.sum((patch_starts[None, :] <= last[:, None]).astype(jnp.int32), axis=1)]
    convert_element_type x1 -> x0, other arithmetic: 0.8 us -> none  [local(): (byte_states[ROWS - 3:].astype(F32) + fetched.astype(F32)).astype(BF16)]
  transfers between devices with their start and end apart: 1 -> 0, of which waited for: 1 -> 0; matrix products, arithmetic and copies ran while one was open for 1% -> 0% of each run, Pallas kernels for 0% -> 0%
where the time goes in v2:
time: 55.3 us; the launch traced here: 55 us
  Pallas kernels  52.7 us (95%)
  local copies, waits for them, and re-layouts  2.26 us (4%)
    pallas_call x1, Pallas kernels, local(): pl.pallas_call(functools.partial(kernel, outer_count, inner_count), in_sp...  52.7 us
    unnamed x1, local copies, waits for them, and re-layouts  2.26 us

profile of v2, /device:TPU:17, one launch (start us, length us, event | category | flops | bytes accessed | tf_op | source)
XLA Modules:
  0.0 55.0 jit_solution(9662683091188997830)
XLA Ops:
  0.0 52.7 %shard_map.82 = bf16[512,1024]{1,0:T(8,128)(2,1)} custom-call(bf16[512,1024]{1,0:T(8,128)(2,1)} %bytes_hbm.1, bf16[128,1024]{1,0:T(8,128)(2,1)} %patches_hbm.1, s32[1,128]{1,0:T(1,128)} %bitcast.5, s32[8,512]{1,0:T(8,128)} %bitcast.3, bf16[1024,3072]{1,0:T(8,128)(2,1)} %w_hbm.1, f32[4,3072]{1,0:T(4,128)} %taps_ref.1, f32[1,1024]{1,0:T(1,128)} %bitcast.4, ...), custom_call_target="tpu_custom_call" | custom-call | tf_op jit(solution)/shard_map/pallas_call | solution.py:349
  52.7 2.3 %copy.10 = bf16[512,1024]{1,0:T(8,128)(2,1)} copy(bf16[512,1024]{1,0:T(8,128)(2,1)} %shard_map.82) | data formatting | bytes 2097152

commit v3 on v2

--- a/solution.py
+++ b/solution.py
@@ -13,6 +13,8 @@
 ROWS = 512
 PATCHES = 128
 CHUNK = 128
+FINISH = 256
+PIECES = 4
 RIM = 16
 HALF_ROWS = ROWS // 2
 GROUP = HEADS // 2
@@ -62,6 +64,27 @@
     return solved
 
 
+def halves_of(x):
+    high = x.astype(BF16)
+    return high, (x - high.astype(F32)).astype(BF16)
+
+
+def gram_of(k):
+    high, low = halves_of(k)
+    crossed = mm_nt(jnp.concatenate([high, low], axis=1), jnp.concatenate([low, high], axis=1))
+    return mm_nt(high, high) + crossed
+
+
+def role_of(inner):
+    z, x = inner // 4, inner % 4
+    return (x + z) % 2 * HEADS + z * 2 + x // 2
+
+
+def inner_of(role):
+    z = role % HEADS // 2
+    return z * 4 + role % 2 * 2 + (role // HEADS + z) % 2
+
+
 def joined(earlier, later):
     return earlier + later + mm(earlier, later[:HEAD])
 
@@ -71,11 +94,12 @@
     bytes_hbm, patches_hbm, starts_ref, codes_ref, w_hbm, taps_ref, gain_ref, wout_hbm, out_ref,
     hidden, patches, weights, wout, rim_out, rim_in, betas, ext_k, ext_v, ext_q, unit_keys, solved_ref,
     firsts, pairs, moves, slots, before, tree, total, totals, states, landed, qe, oe,
-    sem_in, sem_rim, sem_a, recv_a, sem_b, recv_b, sem_c, recv_c,
+    mixed, sem_in, sem_out, sem_rim, sem_a, recv_a, sem_b, recv_b, sem_c, recv_c,
 ):
     outer = lax.axis_index("outer")
     inner = lax.axis_index("inner")
     place = outer * inner_count + inner
+    mine = role_of(inner)
     devices = outer_count * inner_count
 
     loads = [
@@ -89,7 +113,7 @@
             )
         )
     loads.append(pltpu.make_async_copy(wout_hbm, wout, sem_in.at[8]))
-    for load in loads:
+    for load in loads[:2]:
         load.start()
 
     barrier = pltpu.get_barrier_semaphore()
@@ -107,6 +131,9 @@
     for step in range(1, outer_count):
         peer = lax.rem(outer + step, outer_count)
         pl.semaphore_signal(barrier, inc=1, device_id=(peer, inner), device_id_type=MESH)
+
+    for load in loads[2:]:
+        load.start()
 
     starts = starts_ref[...]
     rows, cols = grid_of((ROWS, PATCHES))
@@ -119,25 +146,27 @@
         betas[group] = turned.T
     loads[0].wait()
     loads[1].wait()
-    picked = jnp.dot(chosen, patches[...], preferred_element_type=F32)
-    hidden[RIM:, :] = (hidden[RIM:, :].astype(F32) + picked).astype(BF16)
+    tail = hidden[ROWS:, :].astype(F32) + jnp.dot(chosen[ROWS - RIM :], patches[...], preferred_element_type=F32)
     rim_rows, _ = grid_of((RIM, WIDTH))
-    rim_out[...] = jnp.where(
-        rim_rows == RIM - 4, patches[PATCHES - 1 :, :].astype(F32), hidden[ROWS:, :].astype(F32)
-    ).astype(BF16)
+    rim_out[...] = jnp.where(rim_rows == RIM - 4, patches[PATCHES - 1 :, :].astype(F32), tail).astype(BF16)
     pl.semaphore_wait(barrier, inner_count + outer_count)
     rim_copy = pltpu.make_async_remote_copy(
         src_ref=rim_out, dst_ref=rim_in, send_sem=sem_rim.at[0], recv_sem=sem_rim.at[1],
         device_id=following, device_id_type=MESH,
     )
     rim_copy.start()
+    picked = jnp.dot(chosen, patches[...], preferred_element_type=F32)
+    hidden[RIM:, :] = (hidden[RIM:, :].astype(F32) + picked).astype(BF16)
     for load in loads[2:6]:
         load.wait()
     rim_copy.wait_recv()
     rim = jnp.where(place > 0, rim_in[...].astype(F32), 0.0)
     hidden[:RIM, :] = rim.astype(BF16)
-    filled = hidden[RIM:, :].astype(F32)
-    hidden[RIM:, :] = jnp.where(open_rows, filled + rim[RIM - 4 : RIM - 3, :], filled).astype(BF16)
+    can_be_open = pl.ds(RIM, ROWS - PATCHES)
+    filled = hidden[can_be_open, :].astype(F32)
+    hidden[can_be_open, :] = jnp.where(
+        open_rows[: ROWS - PATCHES], filled + rim[RIM - 4 : RIM - 3, :], filled
+    ).astype(BF16)
 
     def activate(part, row_half, group, ext):
         here = hidden[pl.ds(pl.multiple_of(row_half * HALF_ROWS, HALF_ROWS), HALF_ROWS + RIM), :]
@@ -154,17 +183,17 @@
     def spread(role):
         return pltpu.make_async_remote_copy(
             src_ref=moves.at[role], dst_ref=slots.at[inner], send_sem=sem_a.at[role], recv_sem=recv_a.at[inner],
-            device_id=(outer, role), device_id_type=MESH,
+            device_id=(outer, inner_of(role)), device_id_type=MESH,
         )
 
     def spread_from(source):
         return pltpu.make_async_remote_copy(
-            src_ref=moves.at[source], dst_ref=slots.at[source], send_sem=sem_a.at[source], recv_sem=recv_a.at[source],
-            device_id=(outer, source), device_id_type=MESH,
+            src_ref=moves.at[role_of(source)], dst_ref=slots.at[source], send_sem=sem_a.at[role_of(source)],
+            recv_sem=recv_a.at[source], device_id=(outer, source), device_id_type=MESH,
         )
 
     def critical(step, _):
-        row_half, group = 1 - step // 2, lax.rem(step, 2)
+        row_half, group = 1 - lax.rem(step, 2), step // 2
         keys = activate(1, row_half, group, ext_k)
         values = activate(2, row_half, group, ext_v)
         beta = betas[group, pl.ds(pl.multiple_of(row_half * HALF_ROWS, HALF_ROWS), HALF_ROWS), :]
@@ -177,13 +206,16 @@
             for c in range(2):
                 part = slice(c * CHUNK, (c + 1) * CHUNK)
                 items.append((k[part], values[part, span], beta[part, head : head + 1]))
-        lowers = [jnp.where(tile_rows > tile_cols, beta * mm_nt(k, k), 0.0) for k, _, beta in items]
+        lowers = [jnp.where(tile_rows > tile_cols, beta * gram_of(k), 0.0) for k, _, beta in items]
         inverses = unit_lower_inverses(lowers)
-        solved = [
-            mm(x, jnp.concatenate([-beta * k, beta * v], axis=1)).astype(BF16)
-            for x, (k, v, beta) in zip(inverses, items)
+        sides = [jnp.concatenate([-beta * k, beta * v], axis=1) for k, v, beta in items]
+        rough = [mm(x, side).astype(BF16) for x, side in zip(inverses, sides)]
+        missed = [
+            side - z.astype(F32) - mm(jnp.concatenate(halves_of(low), axis=1), jnp.concatenate([z, z], axis=0))
+            for z, low, side in zip(rough, lowers, sides)
         ]
-        parts = [mm(k.T, s) for (k, _, _), s in zip(items, solved)]
+        solved = [(z.astype(F32) + mm(x, left)).astype(BF16) for z, x, left in zip(rough, inverses, missed)]
+        parts = [mm(k.astype(BF16).T, s) for (k, _, _), s in zip(items, solved)]
         for head in range(GROUP):
             first, second = parts[2 * head], parts[2 * head + 1]
             for c in range(2):
@@ -196,8 +228,8 @@
             for head in range(GROUP):
                 early, late = pairs[0, group, head], pairs[1, group, head]
                 whole = early + late + mm(late[:, :HEAD], early)
-                move = whole[:, :HEAD].T.astype(BF16)
-                rest = whole[:, HEAD:].T.astype(BF16)
+                flipped = whole.astype(BF16).T
+                move, rest = flipped[:HEAD], flipped[HEAD:]
                 for half in range(2):
                     role = (group * GROUP + head) * 2 + half
                     moves[role, :HEAD, :] = move
@@ -206,11 +238,11 @@
             for at in range(2 * GROUP):
                 role = group * 2 * GROUP + at
 
-                @pl.when(role != inner)
+                @pl.when(role != mine)
                 def _():
                     spread(role).start()
 
-                @pl.when(role == inner)
+                @pl.when(role == mine)
                 def _():
                     slots[inner] = moves[role]
 
@@ -289,21 +321,21 @@
 
     def give(peer):
         return pltpu.make_async_remote_copy(
-            src_ref=states.at[peer], dst_ref=landed.at[inner], send_sem=sem_c.at[peer], recv_sem=recv_c.at[inner],
+            src_ref=states.at[peer], dst_ref=landed.at[mine], send_sem=sem_c.at[peer], recv_sem=recv_c.at[mine],
             device_id=(outer, peer), device_id_type=MESH,
         )
 
     def give_from(source):
         return pltpu.make_async_remote_copy(
-            src_ref=states.at[source], dst_ref=landed.at[source], send_sem=sem_c.at[source],
-            recv_sem=recv_c.at[source], device_id=(outer, source), device_id_type=MESH,
+            src_ref=states.at[source], dst_ref=landed.at[role_of(source)], send_sem=sem_c.at[source],
+            recv_sem=recv_c.at[role_of(source)], device_id=(outer, source), device_id_type=MESH,
         )
 
     for step in range(1, inner_count + 1):
         peer = lax.rem(inner + step, inner_count)
         at_start = (s + mm(s, before[peer, :HEAD, :]) + before[peer, HEAD:, :].astype(F32)).astype(BF16)
         if step == inner_count:
-            landed[inner] = at_start
+            landed[mine] = at_start
         else:
             states[peer] = at_start
             give(peer).start()
@@ -311,8 +343,9 @@
     for step in range(1, inner_count):
         give_from(lax.rem(inner + step, inner_count)).wait_recv()
 
-    def finish(tile, _):
-        at = pl.ds(pl.multiple_of(tile * CHUNK, CHUNK), CHUNK)
+    written = []
+    for tile in range(ROWS // FINISH):
+        at = slice(tile * FINISH, (tile + 1) * FINISH)
         parts = []
         for head in range(HEADS):
             state = jnp.concatenate([landed[2 * head], landed[2 * head + 1]], axis=0)
@@ -322,11 +355,12 @@
             gain = gain_ref[:, head * HEAD : (head + 1) * HEAD]
             parts.append((result * lax.rsqrt(mean + EPS) * gain).astype(BF16))
         normed = jnp.concatenate(parts, axis=1)
-        out_ref[at, :] = jnp.dot(normed, wout[...], preferred_element_type=F32).astype(BF16)
-        return 0
-
-    lax.fori_loop(0, ROWS // CHUNK, finish, 0)
-
+        mixed[at, :] = jnp.dot(normed, wout[...], preferred_element_type=F32).astype(BF16)
+        written.append(pltpu.make_async_copy(mixed.at[at], out_ref.at[at], sem_out.at[tile]))
+        written[-1].start()
+
+    for copy in written:
+        copy.wait()
     rim_copy.wait_send()
     for step in range(1, inner_count):
         peer = lax.rem(inner + step, inner_count)
@@ -340,16 +374,29 @@
             outward(peer).wait_send()
 
 
+def copy_kernel(from_ref, to_ref, held, sem_from, sem_to):
+    pieces = [pl.ds(at * (ROWS // PIECES), ROWS // PIECES) for at in range(PIECES)]
+    arriving = [pltpu.make_async_copy(from_ref.at[p], held.at[p], sem_from.at[at]) for at, p in enumerate(pieces)]
+    leaving = [pltpu.make_async_copy(held.at[p], to_ref.at[p], sem_to.at[at]) for at, p in enumerate(pieces)]
+    for copy in arriving:
+        copy.start()
+    for first, second in zip(arriving, leaving):
+        first.wait()
+        second.start()
+    for copy in leaving:
+        copy.wait()
+
+
 def local(byte_states, patch_vectors, patch_starts, beta_codes, w_qkv, conv_taps, norm_gain, w_out):
     outer_count, inner_count = lax.axis_size("outer"), lax.axis_size("inner")
     dma = lambda *n: pltpu.SemaphoreType.DMA(n)
     vmem = lambda *shape: pltpu.VMEM(shape, BF16)
     wide = lambda *shape: pltpu.VMEM(shape, F32)
     here, far = pl.BlockSpec(memory_space=pltpu.VMEM), pl.BlockSpec(memory_space=pl.ANY)
-    return pl.pallas_call(
+    mixed = pl.pallas_call(
         functools.partial(kernel, outer_count, inner_count),
         in_specs=[far, far, here, here, far, here, here, far],
-        out_specs=here,
+        out_specs=far,
         out_shape=jax.ShapeDtypeStruct((ROWS, WIDTH), BF16),
         scratch_shapes=[
             vmem(RIM + ROWS, WIDTH),
@@ -376,7 +423,8 @@
             vmem(inner_count, HALF, HEAD),
             vmem(2, GROUP, ROWS, HEAD),
             wide(2, GROUP, ROWS, HEAD),
-            dma(9), dma(2),
+            vmem(ROWS, WIDTH),
+            dma(9), dma(ROWS // FINISH), dma(2),
             dma(inner_count), dma(inner_count), dma(outer_count), dma(outer_count), dma(inner_count), dma(inner_count),
         ],
         compiler_params=pltpu.CompilerParams(
@@ -386,6 +434,14 @@
         byte_states, patch_vectors, patch_starts.reshape(1, PATCHES), beta_codes.T, w_qkv, conv_taps,
         norm_gain.reshape(1, WIDTH), w_out,
     )
+    return pl.pallas_call(
+        copy_kernel,
+        in_specs=[far],
+        out_specs=far,
+        out_shape=jax.ShapeDtypeStruct((ROWS, WIDTH), BF16),
+        scratch_shapes=[vmem(ROWS, WIDTH), dma(PIECES), dma(PIECES)],
+        compiler_params=pltpu.CompilerParams(vmem_limit_bytes=63 << 20),
+    )(mixed)
 
 
 def solution(mesh):

time: 55.3 us -> 55.5 us (level)
  Pallas kernels: 52.7 us -> 55.3 us
  local copies, waits for them, and re-layouts: 2.26 us -> 0 us
    unnamed x1 -> x0, local copies, waits for them, and re-layouts: 2.26 us -> none
    pallas_call x0 -> x1, Pallas kernels: none -> 1.98 us  [local(): pl.pallas_call(copy_kernel, in_specs=[far], out_specs=far, out_shape=jax....]
    pallas_call x1, Pallas kernels: 52.7 us -> 53.3 us  [local(): pl.pallas_call(functools.partial(kernel, outer_count, inner_count), in_sp...]
where the time goes in v3:
time: 55.5 us; the launch traced here: 55.3 us
  Pallas kernels  55.3 us (100%)
    pallas_call x1, Pallas kernels, local(): pl.pallas_call(functools.partial(kernel, outer_count, inner_count), in_sp...  53.3 us
    pallas_call x1, Pallas kernels, local(): pl.pallas_call(copy_kernel, in_specs=[far], out_specs=far, out_shape=jax....  1.98 us

profile of v3, /device:TPU:17, one launch (start us, length us, event | category | flops | bytes accessed | tf_op | source)
XLA Modules:
  0.0 55.3 jit_solution(1029494403134021077)
XLA Ops:
  0.0 53.3 %shard_map.82.from_ref = bf16[512,1024]{1,0:T(8,128)(2,1)} custom-call(bf16[512,1024]{1,0:T(8,128)(2,1)} %bytes_hbm.1, bf16[128,1024]{1,0:T(8,128)(2,1)} %patches_hbm.1, s32[1,128]{1,0:T(1,128)} %bitcast.5, s32[8,512]{1,0:T(8,128)} %bitcast.3, bf16[1024,3072]{1,0:T(8,128)(2,1)} %w_hbm.1, f32[4,3072]{1,0:T(4,128)} %taps_ref.1, f32[1,1024]{1,0:T(1,128)} %bitcast.4, ...), custom_call_target="tpu_custom_call" | custom-call | tf_op jit(solution)/shard_map/pallas_call | solution.py:396
  53.3 2.0 %shard_map.83 = bf16[512,1024]{1,0:T(8,128)(2,1)} custom-call(bf16[512,1024]{1,0:T(8,128)(2,1)} %shard_map.82.from_ref), custom_call_target="tpu_custom_call" | custom-call | tf_op jit(solution)/shard_map/pallas_call | solution.py:437

commit v4 on v3

--- a/solution.py
+++ b/solution.py
@@ -192,11 +192,10 @@
             recv_sem=recv_a.at[source], device_id=(outer, source), device_id_type=MESH,
         )
 
-    def critical(step, _):
-        row_half, group = 1 - lax.rem(step, 2), step // 2
-        keys = activate(1, row_half, group, ext_k)
-        values = activate(2, row_half, group, ext_v)
-        beta = betas[group, pl.ds(pl.multiple_of(row_half * HALF_ROWS, HALF_ROWS), HALF_ROWS), :]
+    def advance(row_half, group):
+        keys = activate(1, row_half, group, ext_k.at[row_half])
+        values = activate(2, row_half, group, ext_v.at[row_half])
+        beta = betas[group, row_half * HALF_ROWS : (row_half + 1) * HALF_ROWS, :]
         items = []
         for head in range(GROUP):
             span = slice(head * HEAD, (head + 1) * HEAD)
@@ -223,32 +222,35 @@
             firsts[row_half, group, head] = first.astype(BF16)
             pairs[row_half, group, head] = first + second + mm(second[:, :HEAD], first)
 
-        @pl.when(row_half == 0)
-        def _():
-            for head in range(GROUP):
-                early, late = pairs[0, group, head], pairs[1, group, head]
-                whole = early + late + mm(late[:, :HEAD], early)
-                flipped = whole.astype(BF16).T
-                move, rest = flipped[:HEAD], flipped[HEAD:]
-                for half in range(2):
-                    role = (group * GROUP + head) * 2 + half
-                    moves[role, :HEAD, :] = move
-                    moves[role, HEAD:, :] = rest[half * HALF : (half + 1) * HALF]
-
-            for at in range(2 * GROUP):
-                role = group * 2 * GROUP + at
-
-                @pl.when(role != mine)
-                def _():
-                    spread(role).start()
-
-                @pl.when(role == mine)
-                def _():
-                    slots[inner] = moves[role]
-
+    def send(group):
+        for head in range(GROUP):
+            early, late = pairs[0, group, head], pairs[1, group, head]
+            whole = early + late + mm(late[:, :HEAD], early)
+            flipped = whole.astype(BF16).T
+            move, rest = flipped[:HEAD], flipped[HEAD:]
+            for half in range(2):
+                role = (group * GROUP + head) * 2 + half
+                moves[role, :HEAD, :] = move
+                moves[role, HEAD:, :] = rest[half * HALF : (half + 1) * HALF]
+
+        for at in range(2 * GROUP):
+            role = group * 2 * GROUP + at
+
+            @pl.when(role != mine)
+            def _():
+                spread(role).start()
+
+            @pl.when(role == mine)
+            def _():
+                slots[inner] = moves[role]
+
+    def critical(group, _):
+        advance(1, group)
+        advance(0, group)
+        send(group)
         return 0
 
-    lax.fori_loop(0, 4, critical, 0)
+    lax.fori_loop(0, 2, critical, 0)
 
     for load in loads[6:8]:
         load.wait()
@@ -406,8 +408,8 @@
             vmem(RIM, WIDTH),
             vmem(RIM, WIDTH),
             wide(2, ROWS, GROUP),
-            wide(RIM + HALF_ROWS, COLS),
-            wide(RIM + HALF_ROWS, COLS),
+            wide(2, RIM + HALF_ROWS, COLS),
+            wide(2, RIM + HALF_ROWS, COLS),
             wide(RIM + HALF_ROWS, COLS),
             vmem(2, 2, GROUP, HALF_ROWS, HEAD),
             vmem(2, 2, GROUP, 2, CHUNK, 2 * HEAD),

time: 55.5 us -> 54.6 us (0.984)
  Pallas kernels: 55.3 us -> 54.4 us
    pallas_call x1, Pallas kernels: 53.3 us -> 52.4 us  [local(): pl.pallas_call(functools.partial(kernel, outer_count, inner_count), in_sp...]
where the time goes in v4:
time: 54.6 us; the launch traced here: 54.4 us
  Pallas kernels  54.4 us (100%)
    pallas_call x1, Pallas kernels, local(): pl.pallas_call(functools.partial(kernel, outer_count, inner_count), in_sp...  52.4 us
    pallas_call x1, Pallas kernels, local(): pl.pallas_call(copy_kernel, in_specs=[far], out_specs=far, out_shape=jax....  1.98 us

profile of v4, /device:TPU:17, one launch (start us, length us, event | category | flops | bytes accessed | tf_op | source)
XLA Modules:
  0.0 54.4 jit_solution(7622710132051016566)
XLA Ops:
  0.0 52.4 %shard_map.82.from_ref = bf16[512,1024]{1,0:T(8,128)(2,1)} custom-call(bf16[512,1024]{1,0:T(8,128)(2,1)} %bytes_hbm.1, bf16[128,1024]{1,0:T(8,128)(2,1)} %patches_hbm.1, s32[1,128]{1,0:T(1,128)} %bitcast.5, s32[8,512]{1,0:T(8,128)} %bitcast.3, bf16[1024,3072]{1,0:T(8,128)(2,1)} %w_hbm.1, f32[4,3072]{1,0:T(4,128)} %taps_ref.1, f32[1,1024]{1,0:T(1,128)} %bitcast.4, ...), custom_call_target="tpu_custom_call" | custom-call | tf_op jit(solution)/shard_map/pallas_call | solution.py:398
  52.4 2.0 %shard_map.83 = bf16[512,1024]{1,0:T(8,128)(2,1)} custom-call(bf16[512,1024]{1,0:T(8,128)(2,1)} %shard_map.82.from_ref), custom_call_target="tpu_custom_call" | custom-call | tf_op jit(solution)/shard_map/pallas_call | solution.py:439

commit v5 on v4

--- a/solution.py
+++ b/solution.py
@@ -55,12 +55,16 @@
     eye = (rows == cols).astype(F32)
     first = level_mask(rows, cols, 1)
     solved = [(eye - jnp.where(first, low, 0.0)) for low in lowers]
-    block = 2
-    while block < CHUNK:
-        mask = level_mask(rows, cols, block)
-        halves = [mm(x, jnp.where(mask, low, 0.0)) for x, low in zip(solved, lowers)]
-        solved = [x - mm(half, x) for half, x in zip(halves, solved)]
-        block *= 2
+    for block, growth in ((2, 2), (4, 4), (16, 4), (64, 2)):
+        size = block * growth
+        mask = (rows // size == cols // size) & (rows // block > cols // block)
+        steps = [mm(x, jnp.where(mask, low, 0.0)) for x, low in zip(solved, lowers)]
+        if growth == 2:
+            solved = [x - mm(step, x) for step, x in zip(steps, solved)]
+        else:
+            both = [mm(step, jnp.concatenate([step, x], axis=1)) for step, x in zip(steps, solved)]
+            once = [x - pair[:, CHUNK:] for x, pair in zip(solved, both)]
+            solved = [part + mm(pair[:, :CHUNK], part) for part, pair in zip(once, both)]
     return solved
 
 

time: 54.6 us -> 54.4 us (level)
  no operation moved by 1% of the time
where the time goes in v5:
time: 54.4 us; the launch traced here: 54.3 us
  Pallas kernels  54.3 us (100%)
    pallas_call x1, Pallas kernels, local(): pl.pallas_call(functools.partial(kernel, outer_count, inner_count), in_sp...  52.3 us
    pallas_call x1, Pallas kernels, local(): pl.pallas_call(copy_kernel, in_specs=[far], out_specs=far, out_shape=jax....  1.98 us

profile of v5, /device:TPU:17, one launch (start us, length us, event | category | flops | bytes accessed | tf_op | source)
XLA Modules:
  0.0 54.3 jit_solution(6280411938752264252)
XLA Ops:
  0.0 52.3 %shard_map.82.from_ref = bf16[512,1024]{1,0:T(8,128)(2,1)} custom-call(bf16[512,1024]{1,0:T(8,128)(2,1)} %bytes_hbm.1, bf16[128,1024]{1,0:T(8,128)(2,1)} %patches_hbm.1, s32[1,128]{1,0:T(1,128)} %bitcast.5, s32[8,512]{1,0:T(8,128)} %bitcast.3, bf16[1024,3072]{1,0:T(8,128)(2,1)} %w_hbm.1, f32[4,3072]{1,0:T(4,128)} %taps_ref.1, f32[1,1024]{1,0:T(1,128)} %bitcast.4, ...), custom_call_target="tpu_custom_call" | custom-call | tf_op jit(solution)/shard_map/pallas_call | solution.py:402
  52.3 2.0 %shard_map.83 = bf16[512,1024]{1,0:T(8,128)(2,1)} custom-call(bf16[512,1024]{1,0:T(8,128)(2,1)} %shard_map.82.from_ref), custom_call_target="tpu_custom_call" | custom-call | tf_op jit(solution)/shard_map/pallas_call | solution.py:443
